TPU v7x, 128 devices: a whole 4x4x4 slice. The times are simulated.
128 devices in a mesh: pool: 4 (over x), ep: 32 (over y, z, core).
Axes of the slice: x: 4, y: 4, z: 4, core: 2. Of those that a mesh axis runs over, the one named last changes fastest.
Arguments:
- tokens: bfloat16 [16384, 4096], P(('pool', 'ep')), may hold values from -6 to 6
- modality: int32 [16384], P(('pool', 'ep')), may hold values from 0 to 1, as said below
- chosen: int32 [32, 512], replicated, may hold values from 0 to 16383, as said below
- gates: float32 [32, 512], P('ep'), may hold values from 0.1 to 1
- w_gate: bfloat16 [32, 4096, 1024], P('ep', None, 'pool'), may hold values from -0.09375 to 0.09375
- w_up: bfloat16 [32, 4096, 1024], P('ep', None, 'pool'), may hold values from -0.09375 to 0.09375
- w_down: bfloat16 [32, 1024, 4096], P('ep', 'pool'), may hold values from -0.1875 to 0.1875
- cotangent: bfloat16 [16384, 4096], P(('pool', 'ep')), may hold values from -6 to 6
Outputs:
- mixed: bfloat16 [16384, 4096], P(('pool', 'ep'))
- token_grad: bfloat16 [16384, 4096], P(('pool', 'ep'))
- gate_grad: float32 [32, 512], P('ep')
- w_gate_grad: float32 [32, 4096, 1024], P('ep', None, 'pool')
- w_up_grad: float32 [32, 4096, 1024], P('ep', None, 'pool')
- w_down_grad: float32 [32, 1024, 4096], P('ep', 'pool')
Inputs may be any that keep to these rules, and one draw needn't show every extreme that they name: Every device's 128 tokens (device i holding tokens i * 128 to (i + 1) * 128 - 1) hold at least 8 tokens of each modality. `chosen`: row e lists 512 different tokens in increasing order; at most 8 of a row fall among one device's 128 tokens, and for every row exactly 8 do in some device.
All inputs are finite; a program needn't handle non-finite values.
Results may differ from a plain program's by a relative error of at most 0.0095.
Values may be sent and summed in bfloat16 or wider, within the bound.
No kernel may reach another device: no remote copies, remote signals or barrier semaphores. Data moves between devices by JAX's collectives and lax.ppermute only.
A program may use at most 128 MiB of HBM per device.

v0:
```python
import jax
import jax.numpy as jnp
from jax import lax
from jax.sharding import PartitionSpec as P


def body(tokens, modality, chosen, gates, w_gate, w_up, w_down, cotangent):
    tok_rows, width = tokens.shape
    pool_size = lax.axis_size("pool")
    ep_size = lax.axis_size("ep")
    devices = pool_size * ep_size
    slot_count = 2 * tok_rows // ep_size
    capacity = chosen.shape[1]
    text_count = 3 * ep_size // 4
    source = lax.axis_index("pool") * ep_size + lax.axis_index("ep")
    first_row = source * tok_rows
    below = jnp.sum((chosen < first_row).astype(jnp.int32), axis=1)
    inside = jnp.sum((chosen < first_row + tok_rows).astype(jnp.int32), axis=1) - below
    offsets = jnp.arange(slot_count, dtype=jnp.int32)
    positions = jnp.minimum(below[:, None] + offsets[None, :], capacity - 1)
    local_rows = jnp.take_along_axis(chosen, positions, axis=1) - first_row
    safe_rows = jnp.clip(local_rows, 0, tok_rows - 1)
    token_kind = modality[safe_rows]
    expert_kind = (jnp.arange(ep_size, dtype=jnp.int32) >= text_count).astype(jnp.int32)
    keep = (offsets[None, :] < inside[:, None]) & (token_kind == expert_kind[:, None])
    flat_keep = keep.reshape(ep_size * slot_count)
    flat_safe = safe_rows.reshape(ep_size * slot_count)
    target_rows = jnp.where(flat_keep, flat_safe, tok_rows)
    send_rows = jnp.where(flat_keep[:, None], tokens[flat_safe], jnp.zeros((), jnp.bfloat16))
    send_rows = send_rows.reshape(ep_size, slot_count, width)
    send_grads = jnp.where(flat_keep[:, None], cotangent[flat_safe], jnp.zeros((), jnp.bfloat16))
    send_grads = send_grads.reshape(ep_size, slot_count, width)
    tiled_rows = jnp.broadcast_to(send_rows[None], (pool_size,) + send_rows.shape).reshape(
        devices, slot_count, width
    )
    tiled_grads = jnp.broadcast_to(send_grads[None], (pool_size,) + send_grads.shape).reshape(
        devices, slot_count, width
    )
    got_rows, got_grads = (
        lax.all_to_all(tiled_rows, ("pool", "ep"), split_axis=0, concat_axis=0, tiled=True),
        lax.all_to_all(tiled_grads, ("pool", "ep"), split_axis=0, concat_axis=0, tiled=True),
    )
    expert = lax.axis_index("ep")
    picks = lax.dynamic_slice_in_dim(chosen, expert, 1, 0)[0]
    holder = picks // tok_rows
    bounds = jnp.arange(devices, dtype=jnp.int32) * tok_rows
    starts = jnp.sum((picks[None, :] < bounds[:, None]).astype(jnp.int32), axis=1)
    slot_of = jnp.arange(capacity, dtype=jnp.int32) - starts[holder]
    flat = holder * slot_count + slot_of
    inputs_e = got_rows.reshape(devices * slot_count, width)[flat]
    grads_e = got_grads.reshape(devices * slot_count, width)[flat]
    gate_row = gates[0]

    def collect(rows):
        total = jnp.zeros((tok_rows, width), jnp.float32).at[target_rows].add(rows, mode="drop")
        return total.astype(jnp.bfloat16)

    def deliver(values):
        buffer = jnp.zeros((devices * slot_count, width), jnp.bfloat16).at[flat].set(values)
        arrived = lax.all_to_all(
            buffer.reshape(devices, slot_count, width),
            ("pool", "ep"),
            split_axis=0,
            concat_axis=0,
            tiled=True,
        )
        arrived = arrived.reshape(pool_size, ep_size * slot_count, width)
        summed = jnp.sum(arrived, axis=0, dtype=jnp.float32)
        return collect(summed)

    w_gate_local = w_gate[0]
    w_up_local = w_up[0]
    w_down_local = w_down[0]
    gate_pre = jnp.dot(inputs_e, w_gate_local, preferred_element_type=jnp.float32)
    up_pre = jnp.dot(inputs_e, w_up_local, preferred_element_type=jnp.float32)
    sig = jax.nn.sigmoid(gate_pre)
    act = gate_pre * sig
    hidden = (act * up_pre).astype(jnp.bfloat16)
    part = jnp.dot(hidden, w_down_local, preferred_element_type=jnp.float32)
    share_out = (gate_row[:, None] * part).astype(jnp.bfloat16)
    mixed = deliver(share_out)
    gate_local = jnp.sum(grads_e.astype(jnp.float32) * part, axis=1)
    gate_grad = lax.psum(gate_local, "pool")[None, :]
    out_grad = (gate_row[:, None] * grads_e.astype(jnp.float32)).astype(jnp.bfloat16)
    contract_rows = (((0,), (0,)), ((), ()))
    contract_cols = (((1,), (1,)), ((), ()))
    wd_grad = lax.dot_general(hidden, out_grad, contract_rows, preferred_element_type=jnp.float32)
    hidden_grad = lax.dot_general(
        out_grad, w_down_local, contract_cols, preferred_element_type=jnp.float32
    )
    gate_back = (hidden_grad * up_pre * (sig * (1.0 + gate_pre * (1.0 - sig)))).astype(jnp.bfloat16)
    up_back = (hidden_grad * act).astype(jnp.bfloat16)
    share_in = lax.dot_general(
        gate_back, w_gate_local, contract_cols, preferred_element_type=jnp.float32
    )
    share_in = share_in + lax.dot_general(
        up_back, w_up_local, contract_cols, preferred_element_type=jnp.float32
    )
    token_grad = deliver(share_in.astype(jnp.bfloat16))
    wg_grad = lax.dot_general(
        inputs_e, gate_back, contract_rows, preferred_element_type=jnp.float32
    )
    wu_grad = lax.dot_general(inputs_e, up_back, contract_rows, preferred_element_type=jnp.float32)
    return (mixed, token_grad, gate_grad, wg_grad[None], wu_grad[None], wd_grad[None])


def solution(mesh):
    return jax.shard_map(
        body,
        mesh=mesh,
        in_specs=(
            P(("pool", "ep"), None),
            P(("pool", "ep")),
            P(),
            P("ep", None),
            P("ep", None, "pool"),
            P("ep", None, "pool"),
            P("ep", "pool", None),
            P(("pool", "ep"), None),
        ),
        out_specs=(
            P(("pool", "ep"), None),
            P(("pool", "ep"), None),
            P("ep", None),
            P("ep", None, "pool"),
            P("ep", None, "pool"),
            P("ep", "pool", None),
        ),
        check_vma=False,
    )
```

profile of v0, /device:TPU:0, one launch (start us, length us, event | category | flops | bytes accessed | tf_op | source)
XLA Modules:
  0.0 565.0 jit_solution(18317072716022067877)
XLA Ops:
  0.7 1.1 convert_reduce_fusion.4
  1.8 0.1 shift-left_or_fusion
  1.9 0.1 reshape.509
  2.0 2.3 gather_fusion.6
  4.4 0.1 compare_select_fusion
  4.5 0.1 reshape.463
  4.6 0.4 copy-done.2
  5.0 1.9 gather_fusion
  6.9 0.1 reshape.462
  7.0 0.1 add.193
  7.1 0.1 lt.161
  7.3 3.2 gather_fusion.4
  10.4 6.6 %gather_fusion.2 = bf16[256,4096]{1,0:T(8,128)(2,1)} fusion(bf16[128,4096]{1,0:T(8,128)(2,1)} %param.8, s32[1024]{0:T(1024)S(1)} %pad_clamp_fusion.1), kind=kCustom, calls=%fused_computation.2 | custom fusion | bytes 4195328 | tf_op jit(solution)/shard_map/gather | solution.py:29
  17.1 3.9 bitcast_select_fusion
  21.0 2.6 broadcast_in_dim.70
  23.6 109.4 %all_to_all.20 = bf16[128,8,4096]{2,1,0:T(8,128)(2,1)} all-to-all(bf16[128,8,4096]{2,1,0:T(8,128)(2,1)S(1)} %bitcast.81), channel_id=1, replica_groups=mesh['pool'=4,'ep'=32] {'pool','ep'}, dimensions={0} | all-to-all | bytes 16777216 | tf_op jit(solution)/shard_map/all_to_all | solution.py:41
  133.0 4.3 broadcast_in_dim.69
  137.3 8.2 %all-to-all-start = ((bf16[128,8,4096]{2,1,0:T(8,128)(2,1)}), bf16[128,8,4096]{2,1,0:T(8,128)(2,1)}, u32[]{:S(2)}, u32[]{:S(2)}) async-start(bf16[128,8,4096]{2,1,0:T(8,128)(2,1)} %bitcast.80), calls=%async_computation | async-start | bytes 16777216 | tf_op jit(solution)/shard_map/all_to_all | solution.py:40
  145.6 0.2 convert_reduce_fusion.2
  145.7 3.3 gather_fusion.1
  149.1 13.0 %gather_fusion.5 = bf16[512,4096]{1,0:T(8,128)(2,1)} fusion(bf16[1024,4096]{1,0:T(8,128)(2,1)} %bitcast.79, s32[1024]{0:T(1024)S(1)} %pad_clamp_fusion), kind=kCustom, calls=%fused_computation.5 | custom fusion | bytes 8390656 | tf_op jit(solution)/shard_map/gather | solution.py:51
  162.2 85.8 %all-to-all-done = bf16[128,8,4096]{2,1,0:T(8,128)(2,1)} async-done(((bf16[128,8,4096]{2,1,0:T(8,128)(2,1)}), bf16[128,8,4096]{2,1,0:T(8,128)(2,1)}, u32[]{:S(2)}, u32[]{:S(2)}) %all-to-all-start) | async-done | bytes 8388640 | tf_op jit(solution)/shard_map/all_to_all | solution.py:40
  248.0 13.3 %gather_fusion.3 = bf16[512,4096]{1,0:T(8,128)(2,1)} fusion(bf16[1024,4096]{1,0:T(8,128)(2,1)} %bitcast.11, s32[1024]{0:T(1024)S(1)} %pad_clamp_fusion), kind=kCustom, calls=%fused_computation.3 | custom fusion | bytes 8390656 | tf_op jit(solution)/shard_map/gather | solution.py:50
  261.3 4.3 fusion.15
  265.5 0.4 copy-done.8
  266.0 1.2 fusion.11
  267.2 0.9 copy-done.7
  268.2 1.4 multiply_convert_fusion.2
  269.6 4.5 fusion.1
  274.1 3.8 mul.76
  277.9 16.8 %scatter_custom_fusion = bf16[1024,4096]{1,0:T(8,128)(2,1)} fusion(s32[512]{0:T(512)S(1)} %bitcast.89, f32[512,4096]{1,0:T(8,128)} %mul.76, f32[512,4096]{1,0:T(8,128)} %get-tuple-element.19, bf16[]{:T(256)} %constant.35.clone.1), kind=kCustom, calls=%fused_computation.22 | custom fusion | flops 4194304 | bytes 25165826 | tf_op jit(solution)/shard_map/scatter | solution.py:59
  294.7 9.2 %all-to-all-start.1 = ((bf16[128,8,4096]{2,1,0:T(8,128)(2,1)}), bf16[128,8,4096]{2,1,0:T(8,128)(2,1)}, u32[]{:S(2)}, u32[]{:S(2)}) async-start(bf16[128,8,4096]{2,1,0:T(8,128)(2,1)} %bitcast.83), calls=%async_computation.1 | async-start | bytes 16777216 | tf_op jit(solution)/shard_map/all_to_all | solution.py:60
  303.9 3.0 fusion.13
  306.9 3.4 add_convert_fusion
  310.3 12.6 %scatter_custom_fusion.2 = bf16[1024,4096]{1,0:T(8,128)(2,1)} fusion(s32[512]{0:T(512)S(1)} %bitcast.90, bf16[512,4096]{1,0:T(8,128)(2,1)} %add_convert_fusion, bf16[]{:T(256)} %constant.35.clone.1), kind=kCustom, calls=%fused_computation.23 | custom fusion | bytes 8389120 | tf_op jit(solution)/shard_map/scatter | solution.py:59
  322.9 83.4 %all-to-all-done.1 = bf16[128,8,4096]{2,1,0:T(8,128)(2,1)} async-done(((bf16[128,8,4096]{2,1,0:T(8,128)(2,1)}), bf16[128,8,4096]{2,1,0:T(8,128)(2,1)}, u32[]{:S(2)}, u32[]{:S(2)}) %all-to-all-start.1) | async-done | bytes 8388640 | tf_op jit(solution)/shard_map/all_to_all | solution.py:60
  406.3 9.0 %all-to-all-start.3 = ((bf16[128,8,4096]{2,1,0:T(8,128)(2,1)}), bf16[128,8,4096]{2,1,0:T(8,128)(2,1)}, u32[]{:S(2)}, u32[]{:S(2)}) async-start(bf16[128,8,4096]{2,1,0:T(8,128)(2,1)} %bitcast.82), calls=%async_computation.3 | async-start | bytes 16777216 | tf_op jit(solution)/shard_map/all_to_all | solution.py:60
  415.3 0.1 and.76
  415.4 101.0 %psum.7 = f32[1,512]{1,0:T(1,128)} all-reduce(f32[1,512]{1,0:T(1,128)S(1)} %bitcast.94), channel_id=1, replica_groups=mesh['pool'=4,'ep'=32] {'pool'}, use_global_device_ids=true, to_apply=%region_10.11 | all-reduce | flops 512 | bytes 4096 | tf_op jit(solution)/shard_map/psum | solution.py:83
  516.4 5.7 %convolution_bitcast_fusion = f32[1,256,4096]{2,1,0:T(8,128)} fusion(bf16[512,256]{1,0:T(8,128)(2,1)S(1)} %get-tuple-element.15, bf16[512,4096]{1,0:T(8,128)(2,1)} %gather_fusion.5, f32[512]{0:T(512)S(1)} %bitcast.87), kind=kOutput, calls=%fused_computation.19 | convolution fusion | flops 1080033280 | bytes 8652800 | tf_op jit(solution)/shard_map/dot_general | solution.py:87
  522.2 3.3 convolution_bitcast_fusion.2
  525.5 3.3 convolution_bitcast_fusion.1
  528.8 7.3 %convert_reduce_fusion.1 = f32[256,4096]{1,0:T(8,128)} fusion(bf16[4,256,4096]{2,1,0:T(8,128)(2,1)} %bitcast.78), kind=kLoop, calls=%fused_computation.12 | loop fusion | flops 7340032 | bytes 12582912 | tf_op jit(solution)/shard_map/reduce_sum | solution.py:68
  536.1 8.3 %scatter_custom_fusion.1 = f32[128,4096]{1,0:T(8,128)S(1)} fusion(s32[256]{0:T(256)S(1)} %bitcast.96, f32[256,4096]{1,0:T(8,128)} %convert_reduce_fusion.1, f32[]{:T(128)} %constant.19.clone.1), kind=kCustom, calls=%fused_computation.41 | custom fusion | flops 1048576 | bytes 2097664 | tf_op jit(solution)/shard_map/scatter-add | solution.py:55
  544.4 1.1 convert_element_type.64
  545.5 7.5 %convert_reduce_fusion = f32[256,4096]{1,0:T(8,128)} fusion(bf16[4,256,4096]{2,1,0:T(8,128)(2,1)} %bitcast.77), kind=kLoop, calls=%fused_computation.11 | loop fusion | flops 7340032 | bytes 12582912 | tf_op jit(solution)/shard_map/reduce_sum | solution.py:68
  552.9 8.9 %scatter_custom_fusion.3 = f32[128,4096]{1,0:T(8,128)} fusion(s32[256]{0:T(256)S(1)} %bitcast.97, f32[256,4096]{1,0:T(8,128)} %convert_reduce_fusion, f32[]{:T(128)} %constant.19.clone.1), kind=kCustom, calls=%fused_computation.39 | custom fusion | flops 1048576 | bytes 2097664 | tf_op jit(solution)/shard_map/scatter-add | solution.py:55
  561.9 2.7 convert_element_type.72
  (35 shorter events, 0.4 us)
Async XLA Ops:
  0.6 266.6 %copy-start = (bf16[1,256,4096]{2,1,0:T(8,128)(2,1)S(1)}, bf16[1,256,4096]{2,1,0:T(8,128)(2,1)}, u32[]{:S(2)}) copy-start(bf16[1,256,4096]{2,1,0:T(8,128)(2,1)} %param.14) | copy-start | bytes 6291460
  0.6 1.3 copy-start.3
  4.3 0.7 copy-start.2
  5.0 2.3 copy-start.4
  137.3 110.7 %all-to-all-start = ((bf16[128,8,4096]{2,1,0:T(8,128)(2,1)}), bf16[128,8,4096]{2,1,0:T(8,128)(2,1)}, u32[]{:S(2)}, u32[]{:S(2)}) async-start(bf16[128,8,4096]{2,1,0:T(8,128)(2,1)} %bitcast.80), calls=%async_computation | async-start | bytes 16777216 | tf_op jit(solution)/shard_map/all_to_all | solution.py:40
  261.2 4.3 copy-start.5
  261.2 4.7 copy-start.8
  266.0 2.2 copy-start.7
  266.0 2.2 copy-start.10
  294.7 111.6 %all-to-all-start.1 = ((bf16[128,8,4096]{2,1,0:T(8,128)(2,1)}), bf16[128,8,4096]{2,1,0:T(8,128)(2,1)}, u32[]{:S(2)}, u32[]{:S(2)}) async-start(bf16[128,8,4096]{2,1,0:T(8,128)(2,1)} %bitcast.83), calls=%async_computation.1 | async-start | bytes 16777216 | tf_op jit(solution)/shard_map/all_to_all | solution.py:60
  303.9 3.0 copy-start.9
  406.3 139.2 %all-to-all-start.3 = ((bf16[128,8,4096]{2,1,0:T(8,128)(2,1)}), bf16[128,8,4096]{2,1,0:T(8,128)(2,1)}, u32[]{:S(2)}, u32[]{:S(2)}) async-start(bf16[128,8,4096]{2,1,0:T(8,128)(2,1)} %bitcast.82), calls=%async_computation.3 | async-start | bytes 16777216 | tf_op jit(solution)/shard_map/all_to_all | solution.py:60
  516.4 5.7 %copy-start.6 = (bf16[512,4096]{1,0:T(8,128)(2,1)S(1)}, bf16[512,4096]{1,0:T(8,128)(2,1)}, u32[]{:S(2)}) copy-start(bf16[512,4096]{1,0:T(8,128)(2,1)} %gather_fusion.3) | copy-start | bytes 12582916
  545.5 19.1 %copy-start.1 = (bf16[1,256,4096]{2,1,0:T(8,128)(2,1)S(1)}, bf16[1,256,4096]{2,1,0:T(8,128)(2,1)}, u32[]{:S(2)}) copy-start(bf16[1,256,4096]{2,1,0:T(8,128)(2,1)} %param.14) | copy-start | bytes 6291460
where the time goes:
time: 575 us; the launch traced here: 565 us
  blocking collectives  210 us (37%)
  waiting for transfers between devices  169 us (29%)
  local copies, waits for them, and re-layouts  69.4 us (12%)
  other arithmetic  58.1 us (10%)
  matrix products  30.1 us (5%)
  starting transfers between devices  26.4 us (5%)
    all_to_all x1, blocking collectives, body(): lax.all_to_all(tiled_grads, ('pool', 'ep'), split_axis=0, concat_axis=0,...  109 us
    psum x1, blocking collectives, body(): gate_grad = lax.psum(gate_local, 'pool')[None, :]  101 us
    all_to_all x1, waiting for transfers between devices, body(): lax.all_to_all(tiled_rows, ('pool', 'ep'), split_axis=0, concat_axis=0, t...  85.8 us
    all_to_all x2, waiting for transfers between devices, deliver(): lax.all_to_all(buffer.reshape(devices, slot_count, width), ('pool', 'ep')...  83.4 us
    all_to_all x2, starting transfers between devices, deliver(): lax.all_to_all(buffer.reshape(devices, slot_count, width), ('pool', 'ep')...  18.2 us
    scatter-add x2, other arithmetic, collect(): jnp.zeros((tok_rows, width), jnp.float32).at[target_rows]  17.2 us
    scatter x1, other arithmetic, deliver(): jnp.zeros((devices * slot_count, width), jnp.bfloat16).at[flat].set(values)  16.8 us
    reduce_sum x2, other arithmetic, deliver(): summed = jnp.sum(arrived, axis=0, dtype=jnp.float32)  14.8 us
  transfers between devices with their start and end apart: 3, of which 2 were waited for; matrix products, arithmetic and copies ran while one was open for 11% of the time, Pallas kernels for 0%

commit v1 on v0

v1 whole, which is shorter than its diff:
```python
import jax
import jax.numpy as jnp
from jax import lax
from jax.sharding import PartitionSpec as P

BF16 = jnp.bfloat16
F32 = jnp.float32
BOTH = ("pool", "ep")


def dot(a, b, dims, out=F32):
    return lax.dot_general(a, b, ((dims[0], dims[1]), ((), ())), preferred_element_type=out)


def shift(value, step):
    size = lax.axis_size("pool")
    return lax.ppermute(value, "pool", [(i, (i + step) % size) for i in range(size)])


def gather_ring(block):
    rows, cols = block.shape
    half = rows // 2
    me = lax.axis_index("pool")
    size = lax.axis_size("pool")
    left = shift(block, 1)
    right = shift(block, -1)
    far_top = shift(left[:half], 1)
    far_low = shift(right[half:], -1)
    whole = jnp.zeros((rows, size * cols), block.dtype)
    far = jnp.concatenate([far_top, far_low], axis=0)
    for step, piece in ((0, block), (-1, left), (1, right), (2, far)):
        whole = lax.dynamic_update_slice(whole, piece, (0, (me + step) % size * cols))
    return whole


def scatter_ring(whole):
    rows, width = whole.shape
    size = lax.axis_size("pool")
    cols = width // size
    half = rows // 2
    me = lax.axis_index("pool")

    def block(step):
        return lax.dynamic_slice(whole, (0, (me + step) % size * cols), (rows, cols))

    def add(a, b):
        return (a.astype(F32) + b.astype(F32)).astype(BF16)

    far = block(2)
    from_left = shift(far[:half], 1)
    from_right = shift(far[half:], -1)
    ahead, behind = block(1), block(-1)
    from_left = shift(jnp.concatenate([add(ahead[:half], from_left), ahead[half:]], axis=0), 1)
    from_right = shift(jnp.concatenate([behind[:half], add(behind[half:], from_right)], axis=0), -1)
    return (block(0).astype(F32) + from_left.astype(F32) + from_right.astype(F32)).astype(BF16)


def exchange(blocks):
    return lax.all_to_all(blocks, BOTH, split_axis=0, concat_axis=0, tiled=True)


def body(tokens, modality, chosen, gates, w_gate, w_up, w_down, cotangent):
    tok_rows, width = tokens.shape
    pool_size = lax.axis_size("pool")
    ep_size = lax.axis_size("ep")
    devices = pool_size * ep_size
    slots = 2 * tok_rows // ep_size
    capacity = chosen.shape[1]
    text_count = 3 * ep_size // 4
    cols = width // pool_size
    expert = lax.axis_index("ep")
    source = lax.axis_index("pool") * ep_size + expert

    local = chosen - source * tok_rows
    below = jnp.sum((local < 0).astype(jnp.int32), axis=1, keepdims=True)
    inside = (local >= 0) & (local < tok_rows)
    place = jnp.where(inside, jnp.arange(capacity, dtype=jnp.int32)[None, :] - below, -1)
    at_slot = place[:, None, :] == jnp.arange(slots, dtype=jnp.int32)[None, :, None]
    token_at = jnp.sum(jnp.where(at_slot, local[:, None, :] + 1, 0), axis=2) - 1
    token_at = token_at.reshape(ep_size * slots, 1)
    kind = (jnp.arange(ep_size * slots, dtype=jnp.int32) >= text_count * slots).astype(jnp.int32)
    pick = (token_at == jnp.arange(tok_rows, dtype=jnp.int32)[None, :]) & (
        kind[:, None] == modality[None, :]
    )
    pick = pick.astype(BF16)

    picks = lax.dynamic_slice_in_dim(chosen, expert, 1, 0)[0]
    holder = picks // tok_rows
    order = jnp.arange(capacity, dtype=jnp.int32)
    same = (holder[:, None] == holder[None, :]) & (order[None, :] < order[:, None])
    flat = holder * slots + jnp.sum(same.astype(jnp.int32), axis=1)
    place_in = (flat[:, None] == jnp.arange(devices * slots, dtype=jnp.int32)[None, :]).astype(BF16)

    def fetch(rows):
        parts = [
            dot(pick, rows[:, q * cols : (q + 1) * cols], ((1,), (0,)), BF16)
            for q in range(pool_size)
        ]
        got = exchange(jnp.stack(parts).reshape(devices, slots, cols))
        return dot(place_in, got.reshape(devices * slots, cols), ((1,), (0,)), BF16)

    def deliver(block):
        buffer = dot(place_in, block, ((0,), (0,)), BF16)
        got = exchange(buffer.reshape(devices, slots, cols)).reshape(pool_size, -1, cols)
        return jnp.concatenate(
            [dot(pick, got[q], ((0,), (0,)), BF16) for q in range(pool_size)], axis=1
        )

    wg, wu, wd = w_gate[0], w_up[0], w_down[0]
    weight = gates[0][:, None]
    inputs = gather_ring(fetch(tokens))
    grads = gather_ring(fetch(cotangent))

    gate_pre = dot(inputs, wg, ((1,), (0,)))
    up_pre = dot(inputs, wu, ((1,), (0,)))
    sig = jax.nn.sigmoid(gate_pre)
    act = gate_pre * sig
    hidden = (act * up_pre).astype(BF16)
    share_out = (weight * dot(hidden, wd, ((1,), (0,)))).astype(BF16)
    mixed = deliver(scatter_ring(share_out))

    back = dot(grads, wd, ((1,), (1,)))
    gate_grad = lax.psum(jnp.sum(back * hidden.astype(F32), axis=1), "pool")[None, :]
    hidden_grad = weight * back
    gate_back = (hidden_grad * up_pre * (sig * (1.0 + gate_pre * (1.0 - sig)))).astype(BF16)
    up_back = (hidden_grad * act).astype(BF16)
    share_in = dot(gate_back, wg, ((1,), (1,))) + dot(up_back, wu, ((1,), (1,)))
    token_grad = deliver(scatter_ring(share_in.astype(BF16)))

    scaled = (weight * hidden.astype(F32)).astype(BF16)
    wd_grad = dot(scaled, grads, ((0,), (0,)))
    wg_grad = dot(inputs, gate_back, ((0,), (0,)))
    wu_grad = dot(inputs, up_back, ((0,), (0,)))
    return (mixed, token_grad, gate_grad, wg_grad[None], wu_grad[None], wd_grad[None])


def solution(mesh):
    return jax.shard_map(
        body,
        mesh=mesh,
        in_specs=(
            P(BOTH, None),
            P(BOTH),
            P(),
            P("ep", None),
            P("ep", None, "pool"),
            P("ep", None, "pool"),
            P("ep", "pool", None),
            P(BOTH, None),
        ),
        out_specs=(
            P(BOTH, None),
            P(BOTH, None),
            P("ep", None),
            P("ep", None, "pool"),
            P("ep", None, "pool"),
            P("ep", "pool", None),
        ),
        check_vma=False,
    )
```

time: 575 us -> 329 us (0.57); the launches traced: 565 us -> 328 us
  blocking collectives: 210 us -> 42.8 us
  local copies, waits for them, and re-layouts: 69.4 us -> 19 us
  waiting for transfers between devices: 169 us -> 121 us
  other arithmetic: 58.1 us -> 15.7 us
  starting transfers between devices: 26.4 us -> 64.6 us
  matrix products: 30.1 us -> 63.8 us
    all_to_all x3 -> x4, waiting for transfers between devices: 169 us -> 59.3 us  [exchange(): return lax.all_to_all(blocks, BOTH, split_axis=0, concat_axis=0, tiled=True)]
    all_to_all x1 -> x0, blocking collectives: 109 us -> none  [body(): lax.all_to_all(tiled_grads, ('pool', 'ep'), split_axis=0, concat_axis=0,...]
    ppermute x0 -> x16, waiting for transfers between devices: none -> 61.5 us  [shift(): lax.ppermute(value, 'pool', [(i, (i + step) % size) for i in range(size)])]
    psum x1, blocking collectives: 101 us -> 42.8 us  [body(): lax.psum(jnp.sum(back * hidden.astype(F32), axis=1), 'pool')[None, :]]
    gather x10 -> x0, local copies, waits for them, and re-layouts: 43.8 us -> none  [the longest x1 13.3 us: body(): inputs_e = got_rows.reshape(devices * slot_count, width)[flat]]
    dot_general x9 -> x29, matrix products: 30.1 us -> 63.8 us  [dot(): lax.dot_general(a, b, ((dims[0], dims[1]), ((), ())), preferred_element_t...]
    ppermute x0 -> x16, starting transfers between devices: none -> 26.5 us  [shift(): lax.ppermute(value, 'pool', [(i, (i + step) % size) for i in range(size)])]
    scatter-add x2 -> x0, other arithmetic: 17.2 us -> none  [collect(): jnp.zeros((tok_rows, width), jnp.float32).at[target_rows]]
  transfers between devices with their start and end apart: 3 -> 20, of which waited for: 2 -> 8; matrix products, arithmetic and copies ran while one was open for 11% -> 23% of each run, Pallas kernels for 0% -> 0%
where the time goes in v1:
time: 329 us; the launch traced here: 328 us
  waiting for transfers between devices  121 us (37%)
  starting transfers between devices  64.6 us (20%)
  matrix products  63.8 us (19%)
  blocking collectives  42.8 us (13%)
  local copies, waits for them, and re-layouts  19 us (6%)
  other arithmetic  15.7 us (5%)
    dot_general x29, matrix products, dot(): lax.dot_general(a, b, ((dims[0], dims[1]), ((), ())), preferred_element_t...  63.8 us
    ppermute x16, waiting for transfers between devices, shift(): lax.ppermute(value, 'pool', [(i, (i + step) % size) for i in range(size)])  61.5 us
    all_to_all x4, waiting for transfers between devices, exchange(): return lax.all_to_all(blocks, BOTH, split_axis=0, concat_axis=0, tiled=True)  59.3 us
    psum x1, blocking collectives, body(): lax.psum(jnp.sum(back * hidden.astype(F32), axis=1), 'pool')[None, :]  42.8 us
    all_to_all x4, starting transfers between devices, exchange(): return lax.all_to_all(blocks, BOTH, split_axis=0, concat_axis=0, tiled=True)  38.1 us
    ppermute x16, starting transfers between devices, shift(): lax.ppermute(value, 'pool', [(i, (i + step) % size) for i in range(size)])  26.5 us
    dynamic_update_slice x4, local copies, waits for them, and re-layouts, gather_ring(): lax.dynamic_update_slice(whole, piece, (0, (me + step) % size * cols))  8.09 us
  transfers between devices with their start and end apart: 20, of which 8 were waited for; matrix products, arithmetic and copies ran while one was open for 23% of the time, Pallas kernels for 0%

profile of v1, /device:TPU:0, one launch (start us, length us, event | category | flops | bytes accessed | tf_op | source)
XLA Modules:
  0.0 327.8 jit_solution(7510815326337053970)
XLA Ops:
  7.5 1.6 pad_maximum_fusion.1
  9.1 11.7 %all-to-all-start.2 = ((bf16[128,8,1024]{2,1,0:T(8,128)(2,1)}), bf16[128,8,1024]{2,1,0:T(8,128)(2,1)}, u32[]{:S(2)}, u32[]{:S(2)}) async-start(bf16[128,8,1024]{2,1,0:T(8,128)(2,1)} %bitcast.95), calls=%async_computation.2 | async-start | bytes 4194304 | tf_op jit(solution)/shard_map/all_to_all | solution.py:59
  22.2 1.6 pad_maximum_fusion
  23.7 27.2 %all-to-all-done.2 = bf16[128,8,1024]{2,1,0:T(8,128)(2,1)} async-done(((bf16[128,8,1024]{2,1,0:T(8,128)(2,1)}), bf16[128,8,1024]{2,1,0:T(8,128)(2,1)}, u32[]{:S(2)}, u32[]{:S(2)}) %all-to-all-start.2) | async-done | bytes 2097184 | tf_op jit(solution)/shard_map/all_to_all | solution.py:59
  50.9 5.8 %all-to-all-start = ((bf16[128,8,1024]{2,1,0:T(8,128)(2,1)}), bf16[128,8,1024]{2,1,0:T(8,128)(2,1)}, u32[]{:S(2)}, u32[]{:S(2)}) async-start(bf16[128,8,1024]{2,1,0:T(8,128)(2,1)} %bitcast.94), calls=%async_computation | async-start | bytes 4194304 | tf_op jit(solution)/shard_map/all_to_all | solution.py:59
  57.8 2.5 broadcast.105.clone.1
  60.3 4.2 %constant_dynamic-update-slice_fusion.2 = (bf16[512,4096]{1,0:T(8,128)(2,1)}, bf16[512,1024]{1,0:T(8,128)(2,1)}) fusion(bf16[512,4096]{1,0:T(8,128)(2,1)} %broadcast.105.clone.1, s32[]{:T(128)S(6)} %select_n.99, bf16[128,8,1024]{2,1,0:T(8,128)(2,1)} %all-to-all-done.2, s32[512]{0:T(512)S(1)} %multiply_add_fusion), kind=kOutput, calls=%fused_computation.108 | convolution fusion | flops 1074266112 | bytes 4196356 | tf_op jit(solution)/shard_map/dot_general | solution.py:12
  65.2 2.5 collective-permute-start.9
  67.7 19.6 %all-to-all-done = bf16[128,8,1024]{2,1,0:T(8,128)(2,1)} async-done(((bf16[128,8,1024]{2,1,0:T(8,128)(2,1)}), bf16[128,8,1024]{2,1,0:T(8,128)(2,1)}, u32[]{:S(2)}, u32[]{:S(2)}) %all-to-all-start) | async-done | bytes 2097184 | tf_op jit(solution)/shard_map/all_to_all | solution.py:59
  87.4 2.5 broadcast.105.clone
  89.8 4.2 %constant_dynamic-update-slice_fusion.5 = (bf16[512,4096]{1,0:T(8,128)(2,1)}, bf16[512,1024]{1,0:T(8,128)(2,1)}) fusion(bf16[512,4096]{1,0:T(8,128)(2,1)} %broadcast.105.clone, s32[]{:T(128)S(6)} %select_n.99, bf16[128,8,1024]{2,1,0:T(8,128)(2,1)} %all-to-all-done, s32[512]{0:T(512)S(1)} %multiply_add_fusion), kind=kOutput, calls=%fused_computation.114 | convolution fusion | flops 1074266112 | bytes 4196356 | tf_op jit(solution)/shard_map/dot_general | solution.py:12
  94.7 2.6 collective-permute-start.1
  97.3 6.6 %collective-permute-done.8 = bf16[512,1024]{1,0:T(8,128)(2,1)} collective-permute-done((bf16[512,1024]{1,0:T(8,128)(2,1)}, bf16[512,1024]{1,0:T(8,128)(2,1)}, u32[]{:S(2)}, u32[]{:S(2)}) %collective-permute-start.8) | collective-permute-done | bytes 1048608 | tf_op jit(solution)/shard_map/ppermute | solution.py:17
  105.2 3.2 collective-permute-start.11
  108.4 18.0 %collective-permute-done = bf16[512,1024]{1,0:T(8,128)(2,1)} collective-permute-done((bf16[512,1024]{1,0:T(8,128)(2,1)}, bf16[512,1024]{1,0:T(8,128)(2,1)}, u32[]{:S(2)}, u32[]{:S(2)}) %collective-permute-start) | collective-permute-done | bytes 1048608 | tf_op jit(solution)/shard_map/ppermute | solution.py:17
  128.7 3.4 %collective-permute-start.3 = (bf16[256,1024]{1,0:T(8,128)(2,1)S(1)}, bf16[256,1024]{1,0:T(8,128)(2,1)S(1)}, u32[]{:S(2)}, u32[]{:S(2)}) collective-permute-start(bf16[256,1024]{1,0:T(8,128)(2,1)S(1)} %slice.137), channel_id=1, source_target_pairs={{0,96},{32,0},{64,32},{96,64},{1,97},{33,1},{65,33},{97,65},{2,98}... | collective-permute-start | bytes 1572872 | tf_op jit(solution)/shard_map/ppermute | solution.py:17
  132.1 2.3 constant_dynamic-update-slice_fusion.1
  134.4 2.3 constant_dynamic-update-slice_fusion.4
  137.8 2.5 constant_dynamic-update-slice_fusion.3
  140.2 8.2 %collective-permute-done.2 = bf16[256,1024]{1,0:T(8,128)(2,1)S(1)} collective-permute-done((bf16[256,1024]{1,0:T(8,128)(2,1)S(1)}, bf16[256,1024]{1,0:T(8,128)(2,1)S(1)}, u32[]{:S(2)}, u32[]{:S(2)}) %collective-permute-start.2) | collective-permute-done | bytes 524320 | tf_op jit(solution)/shard_map/ppermute | solution.py:17
  149.6 3.6 %fusion.10 = f32[512,256]{0,1:T(8,128)S(1)} fusion(bf16[512,4096]{1,0:T(8,128)(2,1)} %maximum_dynamic-update-slice_fusion, bf16[1,4096,256]{2,1,0:T(8,128)(2,1)S(1)} %copy-done.3), kind=kOutput, calls=%fused_computation.17 | convolution fusion | flops 1073741824 | bytes 6815744 | tf_op jit(solution)/shard_map/dot_general | solution.py:12
  153.3 3.5 %fusion.6 = f32[512,256]{0,1:T(8,128)S(1)} fusion(bf16[512,4096]{1,0:T(8,128)(2,1)} %maximum_dynamic-update-slice_fusion, bf16[1,4096,256]{2,1,0:T(8,128)(2,1)S(1)} %copy-done.2), kind=kOutput, calls=%fused_computation.13 | convolution fusion | flops 1073741824 | bytes 6815744 | tf_op jit(solution)/shard_map/dot_general | solution.py:12
  157.9 3.7 %fusion.25 = (f32[512]{0:T(512)S(1)}, bf16[512,256]{0,1:T(8,128)(2,1)S(1)}, bf16[512,256]{0,1:T(8,128)(2,1)S(1)}, bf16[512,256]{0,1:T(8,128)(2,1)S(1)}) fusion(f32[512,256]{0,1:T(8,128)S(1)} %fusion.6, f32[512,256]{0,1:T(8,128)S(1)} %fusion.10, f32[512]{0:T(512)S(1)} %bitcast.96, bf16[512,4096]{1,0:T(8,128)(2,1)} %maximum_dynamic-update-slice_fusion.1, ...), kind=kOutput, calls=%fused_computation.59 | convolution fusion | flops 1076231680 | bytes 8130560 | tf_op jit(solution)/shard_map/dot_general | solution.py:12
  164.7 3.1 collective-permute-start.14
  167.8 11.6 %collective-permute-done.12 = bf16[256,1024]{1,0:T(8,128)(2,1)S(1)} collective-permute-done((bf16[256,1024]{1,0:T(8,128)(2,1)S(1)}, bf16[256,1024]{1,0:T(8,128)(2,1)S(1)}, u32[]{:S(2)}, u32[]{:S(2)}) %collective-permute-start.12) | collective-permute-done | bytes 524320 | tf_op jit(solution)/shard_map/ppermute | solution.py:17
  180.0 3.3 %collective-permute-start.15 = (bf16[512,1024]{1,0:T(8,128)(2,1)S(1)}, bf16[512,1024]{1,0:T(8,128)(2,1)S(1)}, u32[]{:S(2)}, u32[]{:S(2)}) collective-permute-start(bf16[512,1024]{1,0:T(8,128)(2,1)S(1)} %pad_maximum_fusion.6), channel_id=1, source_target_pairs={{0,96},{32,0},{64,32},{96,64},{1,97},{33,1},{65,33},{97,65},{2,98}... | collective-permute-start | bytes 3145736 | tf_op jit(solution)/shard_map/ppermute | solution.py:17
  184.6 1.4 constant_dynamic-slice_fusion.1
  186.9 3.2 collective-permute-start.6
  190.2 17.1 %collective-permute-done.13 = bf16[512,1024]{1,0:T(8,128)(2,1)S(1)} collective-permute-done((bf16[512,1024]{1,0:T(8,128)(2,1)S(1)}, bf16[512,1024]{1,0:T(8,128)(2,1)S(1)}, u32[]{:S(2)}, u32[]{:S(2)}) %collective-permute-start.13) | collective-permute-done | bytes 1048608 | tf_op jit(solution)/shard_map/ppermute | solution.py:17
  207.2 2.8 fusion.17
  210.1 11.3 %all-to-all-start.3 = ((bf16[128,8,1024]{2,1,0:T(8,128)(2,1)}), bf16[128,8,1024]{2,1,0:T(8,128)(2,1)}, u32[]{:S(2)}, u32[]{:S(2)}) async-start(bf16[128,8,1024]{2,1,0:T(8,128)(2,1)} %fusion.17), calls=%async_computation.3 | async-start | bytes 4194304 | tf_op jit(solution)/shard_map/all_to_all | solution.py:59
  221.4 1.9 add_convert_fusion.8
  226.3 2.4 collective-permute-start.7
  228.7 42.8 %psum.7 = f32[1,512]{1,0:T(1,128)} all-reduce(f32[1,512]{1,0:T(1,128)S(1)} %bitcast.102), channel_id=1, replica_groups=mesh['pool'=4,'ep'=32] {'pool'}, use_global_device_ids=true, to_apply=%region_4.5 | all-reduce | flops 512 | bytes 4096 | tf_op jit(solution)/shard_map/psum | solution.py:123
  271.5 5.5 %convolution_bitcast_fusion.1 = f32[1,4096,256]{2,1,0:T(8,128)} fusion(bf16[512,4096]{1,0:T(8,128)(2,1)} %maximum_dynamic-update-slice_fusion, bf16[512,256]{0,1:T(8,128)(2,1)S(1)} %copy-done.5), kind=kOutput, calls=%fused_computation.3 | convolution fusion | flops 1073741824 | bytes 8650752 | tf_op jit(solution)/shard_map/dot_general | solution.py:12
  277.0 4.6 %fusion.16 = bf16[128,8,1024]{2,1,0:T(8,128)(2,1)} fusion(bf16[512,1024]{1,0:T(8,128)(2,1)} %collective-permute-done.7, bf16[512,1024]{1,0:T(8,128)(2,1)} %collective-permute-done.5, bf16[512,4096]{1,0:T(8,128)(2,1)} %copy-done.1, s32[]{:T(128)S(6)} %select_n.99, s32[512]{0:T(512)S(1)} %multiply_add_fusion), kind=kOutput, calls=%fused_computation.26 | convolution fusion | flops 1077411840 | bytes 5244932 | tf_op jit(solution)/shard_map/dot_general | solution.py:12
  281.6 9.3 %all-to-all-start.1 = ((bf16[128,8,1024]{2,1,0:T(8,128)(2,1)}), bf16[128,8,1024]{2,1,0:T(8,128)(2,1)}, u32[]{:S(2)}, u32[]{:S(2)}) async-start(bf16[128,8,1024]{2,1,0:T(8,128)(2,1)} %fusion.16), calls=%async_computation.1 | async-start | bytes 4194304 | tf_op jit(solution)/shard_map/all_to_all | solution.py:59
  290.9 5.5 %convolution_bitcast_fusion = f32[1,256,4096]{2,1,0:T(8,128)} fusion(bf16[512,4096]{1,0:T(8,128)(2,1)} %maximum_dynamic-update-slice_fusion.1, bf16[512,256]{0,1:T(8,128)(2,1)S(1)} %get-tuple-element.7, f32[512]{0:T(512)S(1)} %bitcast.98), kind=kOutput, calls=%fused_computation.2 | convolution fusion | flops 1074135040 | bytes 8652800 | tf_op jit(solution)/shard_map/dot_general | solution.py:12
  296.5 5.5 %convolution_bitcast_fusion.2 = f32[1,4096,256]{2,1,0:T(8,128)} fusion(bf16[512,4096]{1,0:T(8,128)(2,1)} %maximum_dynamic-update-slice_fusion, bf16[512,256]{0,1:T(8,128)(2,1)S(1)} %copy-done.9), kind=kOutput, calls=%fused_computation.4 | convolution fusion | flops 1073741824 | bytes 8650752 | tf_op jit(solution)/shard_map/dot_general | solution.py:12
  302.0 1.4 fusion.29
  303.4 1.4 fusion.30
  304.8 1.4 fusion.28
  306.2 1.4 fusion.27
  308.7 12.5 %all-to-all-done.1 = bf16[128,8,1024]{2,1,0:T(8,128)(2,1)} async-done(((bf16[128,8,1024]{2,1,0:T(8,128)(2,1)}), bf16[128,8,1024]{2,1,0:T(8,128)(2,1)}, u32[]{:S(2)}, u32[]{:S(2)}) %all-to-all-start.1) | async-done | bytes 2097184 | tf_op jit(solution)/shard_map/all_to_all | solution.py:59
  321.1 1.4 fusion.33
  322.5 1.4 fusion.34
  323.9 1.4 fusion.32
  325.4 1.4 fusion.31
  (80 shorter events, 28.3 us)
Async XLA Ops:
  0.6 157.3 %copy-start = (bf16[1,256,4096]{2,1,0:T(8,128)(2,1)S(1)}, bf16[1,256,4096]{2,1,0:T(8,128)(2,1)}, u32[]{:S(2)}) copy-start(bf16[1,256,4096]{2,1,0:T(8,128)(2,1)} %param.14) | copy-start | bytes 6291460
  0.6 5.5 %copy-start.6 = (bf16[128,4096]{1,0:T(8,128)(2,1)S(1)}, bf16[128,4096]{1,0:T(8,128)(2,1)}, u32[]{:S(2)}) copy-start(bf16[128,4096]{1,0:T(8,128)(2,1)} %param.15) | copy-start | bytes 3145732
  0.7 6.5 %copy-start.11 = (s32[128]{0:T(128)S(1)}, s32[128]{0:T(128)}, u32[]{:S(2)}) copy-start(s32[128]{0:T(128)} %param.9) | copy-start | bytes 1540
  9.1 11.7 %copy-start.7 = (bf16[128,4096]{1,0:T(8,128)(2,1)S(1)}, bf16[128,4096]{1,0:T(8,128)(2,1)}, u32[]{:S(2)}) copy-start(bf16[128,4096]{1,0:T(8,128)(2,1)} %param.8) | copy-start | bytes 3145732
  9.1 41.9 %all-to-all-start.2 = ((bf16[128,8,1024]{2,1,0:T(8,128)(2,1)}), bf16[128,8,1024]{2,1,0:T(8,128)(2,1)}, u32[]{:S(2)}, u32[]{:S(2)}) async-start(bf16[128,8,1024]{2,1,0:T(8,128)(2,1)} %bitcast.95), calls=%async_computation.2 | async-start | bytes 4194304 | tf_op jit(solution)/shard_map/all_to_all | solution.py:59
  50.9 36.4 %all-to-all-start = ((bf16[128,8,1024]{2,1,0:T(8,128)(2,1)}), bf16[128,8,1024]{2,1,0:T(8,128)(2,1)}, u32[]{:S(2)}, u32[]{:S(2)}) async-start(bf16[128,8,1024]{2,1,0:T(8,128)(2,1)} %bitcast.94), calls=%async_computation | async-start | bytes 4194304 | tf_op jit(solution)/shard_map/all_to_all | solution.py:59
  64.5 39.5 %collective-permute-start.8 = (bf16[512,1024]{1,0:T(8,128)(2,1)}, bf16[512,1024]{1,0:T(8,128)(2,1)}, u32[]{:S(2)}, u32[]{:S(2)}) collective-permute-start(bf16[512,1024]{1,0:T(8,128)(2,1)} %get-tuple-element.27), channel_id=1, source_target_pairs={{0,32},{32,64},{64,96},{96,0},{1,33},{33,65},{65,97},{97,1},{2,34}... | collective-permute-start | bytes 3145736 | tf_op jit(solution)/shard_map/ppermute | solution.py:17
  65.2 39.9 %collective-permute-start.9 = (bf16[512,1024]{1,0:T(8,128)(2,1)}, bf16[512,1024]{1,0:T(8,128)(2,1)S(1)}, u32[]{:S(2)}, u32[]{:S(2)}) collective-permute-start(bf16[512,1024]{1,0:T(8,128)(2,1)} %get-tuple-element.27), channel_id=1, source_target_pairs={{0,96},{32,0},{64,32},{96,64},{1,97},{33,1},{65,33},{97,65},{2,98}... | collective-permute-start | bytes 3145736 | tf_op jit(solution)/shard_map/ppermute | solution.py:17
  94.1 32.3 %collective-permute-start = (bf16[512,1024]{1,0:T(8,128)(2,1)}, bf16[512,1024]{1,0:T(8,128)(2,1)}, u32[]{:S(2)}, u32[]{:S(2)}) collective-permute-start(bf16[512,1024]{1,0:T(8,128)(2,1)} %get-tuple-element.29), channel_id=1, source_target_pairs={{0,32},{32,64},{64,96},{96,0},{1,33},{33,65},{65,97},{97,1},{2,34}... | collective-permute-start | bytes 3145736 | tf_op jit(solution)/shard_map/ppermute | solution.py:17
  94.7 33.0 %collective-permute-start.1 = (bf16[512,1024]{1,0:T(8,128)(2,1)}, bf16[512,1024]{1,0:T(8,128)(2,1)}, u32[]{:S(2)}, u32[]{:S(2)}) collective-permute-start(bf16[512,1024]{1,0:T(8,128)(2,1)} %get-tuple-element.29), channel_id=1, source_target_pairs={{0,96},{32,0},{64,32},{96,64},{1,97},{33,1},{65,33},{97,65},{2,98}... | collective-permute-start | bytes 3145736 | tf_op jit(solution)/shard_map/ppermute | solution.py:17
  105.0 51.8 %collective-permute-start.10 = (bf16[256,1024]{1,0:T(8,128)(2,1)S(1)}, bf16[256,1024]{1,0:T(8,128)(2,1)S(1)}, u32[]{:S(2)}, u32[]{:S(2)}) collective-permute-start(bf16[256,1024]{1,0:T(8,128)(2,1)S(1)} %slice.142), channel_id=1, source_target_pairs={{0,32},{32,64},{64,96},{96,0},{1,33},{33,65},{65,97},{97,1},{2,34}... | collective-permute-start | bytes 1572872 | tf_op jit(solution)/shard_map/ppermute | solution.py:17
  105.2 51.6 %collective-permute-start.11 = (bf16[256,1024]{1,0:T(8,128)(2,1)S(1)}, bf16[256,1024]{1,0:T(8,128)(2,1)S(1)}, u32[]{:S(2)}, u32[]{:S(2)}) collective-permute-start(bf16[256,1024]{1,0:T(8,128)(2,1)S(1)} %slice.143), channel_id=1, source_target_pairs={{0,96},{32,0},{64,32},{96,64},{1,97},{33,1},{65,33},{97,65},{2,98}... | collective-permute-start | bytes 1572872 | tf_op jit(solution)/shard_map/ppermute | solution.py:17
  127.5 21.0 %collective-permute-start.2 = (bf16[256,1024]{1,0:T(8,128)(2,1)S(1)}, bf16[256,1024]{1,0:T(8,128)(2,1)S(1)}, u32[]{:S(2)}, u32[]{:S(2)}) collective-permute-start(bf16[256,1024]{1,0:T(8,128)(2,1)S(1)} %slice.136), channel_id=1, source_target_pairs={{0,32},{32,64},{64,96},{96,0},{1,33},{33,65},{65,97},{97,1},{2,34}... | collective-permute-start | bytes 1572872 | tf_op jit(solution)/shard_map/ppermute | solution.py:17
  128.7 19.7 %collective-permute-start.3 = (bf16[256,1024]{1,0:T(8,128)(2,1)S(1)}, bf16[256,1024]{1,0:T(8,128)(2,1)S(1)}, u32[]{:S(2)}, u32[]{:S(2)}) collective-permute-start(bf16[256,1024]{1,0:T(8,128)(2,1)S(1)} %slice.137), channel_id=1, source_target_pairs={{0,96},{32,0},{64,32},{96,64},{1,97},{33,1},{65,33},{97,65},{2,98}... | collective-permute-start | bytes 1572872 | tf_op jit(solution)/shard_map/ppermute | solution.py:17
  137.7 11.9 %copy-start.3 = (bf16[1,4096,256]{2,1,0:T(8,128)(2,1)S(1)}, bf16[1,4096,256]{2,1,0:T(8,128)(2,1)}, u32[]{:S(2)}) copy-start(bf16[1,4096,256]{2,1,0:T(8,128)(2,1)} %param.12) | copy-start | bytes 6291460
  149.6 3.7 %copy-start.2 = (bf16[1,4096,256]{2,1,0:T(8,128)(2,1)S(1)}, bf16[1,4096,256]{2,1,0:T(8,128)(2,1)}, u32[]{:S(2)}) copy-start(bf16[1,4096,256]{2,1,0:T(8,128)(2,1)} %param.13) | copy-start | bytes 6291460
  156.8 1.1 copy-start.10
  161.6 1.3 copy-start.8
  161.6 1.3 copy-start.4
  164.5 14.9 %collective-permute-start.12 = (bf16[256,1024]{1,0:T(8,128)(2,1)S(1)}, bf16[256,1024]{1,0:T(8,128)(2,1)S(1)}, u32[]{:S(2)}, u32[]{:S(2)}) collective-permute-start(bf16[256,1024]{1,0:T(8,128)(2,1)S(1)} %get-tuple-element.12), channel_id=1, source_target_pairs={{0,32},{32,64},{64,96},{96,0},{1,33},{33,65},{65,97},{97,1},{2,34}... | collective-permute-start | bytes 1572872 | tf_op jit(solution)/shard_map/ppermute | solution.py:17
  164.7 14.7 %collective-permute-start.14 = (bf16[256,1024]{1,0:T(8,128)(2,1)S(1)}, bf16[256,1024]{1,0:T(8,128)(2,1)S(1)}, u32[]{:S(2)}, u32[]{:S(2)}) collective-permute-start(bf16[256,1024]{1,0:T(8,128)(2,1)S(1)} %get-tuple-element.14), channel_id=1, source_target_pairs={{0,96},{32,0},{64,32},{96,64},{1,97},{33,1},{65,33},{97,65},{2,98}... | collective-permute-start | bytes 1572872 | tf_op jit(solution)/shard_map/ppermute | solution.py:17
  179.9 27.4 %collective-permute-start.13 = (bf16[512,1024]{1,0:T(8,128)(2,1)S(1)}, bf16[512,1024]{1,0:T(8,128)(2,1)S(1)}, u32[]{:S(2)}, u32[]{:S(2)}) collective-permute-start(bf16[512,1024]{1,0:T(8,128)(2,1)S(1)} %pad_maximum_fusion.5), channel_id=1, source_target_pairs={{0,32},{32,64},{64,96},{96,0},{1,33},{33,65},{65,97},{97,1},{2,34}... | collective-permute-start | bytes 3145736 | tf_op jit(solution)/shard_map/ppermute | solution.py:17
  180.0 27.2 %collective-permute-start.15 = (bf16[512,1024]{1,0:T(8,128)(2,1)S(1)}, bf16[512,1024]{1,0:T(8,128)(2,1)S(1)}, u32[]{:S(2)}, u32[]{:S(2)}) collective-permute-start(bf16[512,1024]{1,0:T(8,128)(2,1)S(1)} %pad_maximum_fusion.6), channel_id=1, source_target_pairs={{0,96},{32,0},{64,32},{96,64},{1,97},{33,1},{65,33},{97,65},{2,98}... | collective-permute-start | bytes 3145736 | tf_op jit(solution)/shard_map/ppermute | solution.py:17
  184.6 2.3 copy-start.1
  186.9 34.5 %collective-permute-start.4 = (bf16[256,1024]{1,0:T(8,128)(2,1)}, bf16[256,1024]{1,0:T(8,128)(2,1)}, u32[]{:S(2)}, u32[]{:S(2)}) collective-permute-start(bf16[256,1024]{1,0:T(8,128)(2,1)} %get-tuple-element.18), channel_id=1, source_target_pairs={{0,32},{32,64},{64,96},{96,0},{1,33},{33,65},{65,97},{97,1},{2,34}... | collective-permute-start | bytes 1572872 | tf_op jit(solution)/shard_map/ppermute | solution.py:17
  186.9 34.5 %collective-permute-start.6 = (bf16[256,1024]{1,0:T(8,128)(2,1)}, bf16[256,1024]{1,0:T(8,128)(2,1)}, u32[]{:S(2)}, u32[]{:S(2)}) collective-permute-start(bf16[256,1024]{1,0:T(8,128)(2,1)} %get-tuple-element.20), channel_id=1, source_target_pairs={{0,96},{32,0},{64,32},{96,64},{1,97},{33,1},{65,33},{97,65},{2,98}... | collective-permute-start | bytes 1572872 | tf_op jit(solution)/shard_map/ppermute | solution.py:17
  210.1 71.6 %all-to-all-start.3 = ((bf16[128,8,1024]{2,1,0:T(8,128)(2,1)}), bf16[128,8,1024]{2,1,0:T(8,128)(2,1)}, u32[]{:S(2)}, u32[]{:S(2)}) async-start(bf16[128,8,1024]{2,1,0:T(8,128)(2,1)} %fusion.17), calls=%async_computation.3 | async-start | bytes 4194304 | tf_op jit(solution)/shard_map/all_to_all | solution.py:59
  224.4 47.1 %copy-start.5 = (bf16[512,256]{0,1:T(8,128)(2,1)S(1)}, bf16[512,256]{0,1:T(8,128)(2,1)}, u32[]{:S(2)}) copy-start(bf16[512,256]{0,1:T(8,128)(2,1)} %copy-done.4) | copy-start | bytes 786436
  224.4 52.6 %collective-permute-start.5 = (bf16[512,1024]{1,0:T(8,128)(2,1)}, bf16[512,1024]{1,0:T(8,128)(2,1)}, u32[]{:S(2)}, u32[]{:S(2)}) collective-permute-start(bf16[512,1024]{1,0:T(8,128)(2,1)} %pad_maximum_fusion.2), channel_id=1, source_target_pairs={{0,32},{32,64},{64,96},{96,0},{1,33},{33,65},{65,97},{97,1},{2,34}... | collective-permute-start | bytes 3145736 | tf_op jit(solution)/shard_map/ppermute | solution.py:17
  226.3 50.7 %collective-permute-start.7 = (bf16[512,1024]{1,0:T(8,128)(2,1)}, bf16[512,1024]{1,0:T(8,128)(2,1)}, u32[]{:S(2)}, u32[]{:S(2)}) collective-permute-start(bf16[512,1024]{1,0:T(8,128)(2,1)} %pad_maximum_fusion.3), channel_id=1, source_target_pairs={{0,96},{32,0},{64,32},{96,64},{1,97},{33,1},{65,33},{97,65},{2,98}... | collective-permute-start | bytes 3145736 | tf_op jit(solution)/shard_map/ppermute | solution.py:17
  281.6 39.5 %all-to-all-start.1 = ((bf16[128,8,1024]{2,1,0:T(8,128)(2,1)}), bf16[128,8,1024]{2,1,0:T(8,128)(2,1)}, u32[]{:S(2)}, u32[]{:S(2)}) async-start(bf16[128,8,1024]{2,1,0:T(8,128)(2,1)} %fusion.16), calls=%async_computation.1 | async-start | bytes 4194304 | tf_op jit(solution)/shard_map/all_to_all | solution.py:59
  290.9 5.5 %copy-start.9 = (bf16[512,256]{0,1:T(8,128)(2,1)S(1)}, bf16[512,256]{0,1:T(8,128)(2,1)}, u32[]{:S(2)}) copy-start(bf16[512,256]{0,1:T(8,128)(2,1)} %copy-done.8) | copy-start | bytes 786436
